TPU v7x, 512 devices: a whole 4x8x8 slice. The times are simulated.
512 devices in a mesh: dp: 64 (over z_lo, y, core), tensor: 8 (over x, z_hi).
Axes of the slice: x: 4, y: 8, z: 8 (z_hi: 2, z_lo: 4; z = z_hi * 4 + z_lo), core: 2. Of those that a mesh axis runs over, the one named last changes fastest.
Arguments:
- tokens: bfloat16 [16384, 2560], P('dp', 'tensor'), may hold values from -6 to 6
- gate_weight: bfloat16 [40960, 6912], P('dp', 'tensor'), may hold values from -0.125 to 0.125
- up_weight: bfloat16 [40960, 6912], P('dp', 'tensor'), may hold values from -0.125 to 0.125
- hidden_grad: bfloat16 [16384, 6912], P('dp', 'tensor'), may hold values from -6 to 6
- step_index: int32 [1], replicated, may hold values from 0 to 999
Outputs:
- averaged_up: bfloat16 [40960, 6912], P('dp', 'tensor')
- input_grad: bfloat16 [16384, 2560], P('dp', 'tensor')
All inputs are finite; a program needn't handle non-finite values.
Results may differ from a plain program's by a relative error of at most 0.013.
Values may be sent and summed in bfloat16 or wider, within the bound.
A program may use at most 128 MiB of HBM per device.

v0:
```python
import jax
import jax.numpy as jnp
from jax import lax
from jax.sharding import PartitionSpec as P


def partner(value, axis, bit):
    mask = 2**bit
    pairs = [(source, source ^ mask) for source in range(lax.axis_size(axis))]
    return lax.ppermute(value, axis, pairs)


def shortened(x):
    return jax.tree.map(lambda a: a.astype(jnp.bfloat16) if a.dtype == jnp.float32 else a, x)


def shifted(x, axis, by):
    devices = lax.axis_size(axis)
    return lax.ppermute(x, axis, [(i, (i + by) % devices) for i in range(devices)])


def place(upper, mine, other):
    return jnp.where(upper, jnp.concatenate([other, mine], 0), jnp.concatenate([mine, other], 0))


def shards(tokens, gate_weight, up_weight, hidden_grad, step_index):
    member = lax.axis_index("dp") % 4
    x_full = lax.all_gather(tokens, "tensor", axis=1, tiled=True)
    gate_w, up_w = (gate_weight, up_weight)
    for level in range(2):
        upper = (member >> level) % 2 == 1
        other_gate, other_up = partner((gate_w, up_w), "dp", level)
        gate_w = place(upper, gate_w, other_gate)
        up_w = place(upper, up_w, other_up)
    gate = jnp.dot(x_full, gate_w, preferred_element_type=jnp.float32)
    up = jnp.dot(x_full, up_w, preferred_element_type=jnp.float32)
    sig = jax.nn.sigmoid(gate)
    cot_wide = hidden_grad.astype(jnp.float32)
    up_delta = (cot_wide * gate * sig).astype(jnp.bfloat16)
    gate_delta = (cot_wide * up * sig * (1.0 + gate * (1.0 - sig))).astype(jnp.bfloat16)
    terms = lax.dot_general(
        up_delta, up_w, (((1,), (1,)), ((), ())), preferred_element_type=jnp.float32
    )
    terms = terms + lax.dot_general(
        gate_delta, gate_w, (((1,), (1,)), ((), ())), preferred_element_type=jnp.float32
    )
    input_grad = lax.psum_scatter(terms, "tensor", scatter_dimension=1, tiled=True).astype(
        jnp.bfloat16
    )
    current = lax.dot_general(
        x_full, up_delta, (((0,), (0,)), ((), ())), preferred_element_type=jnp.float32
    )
    for level in (1, 0):
        size = current.shape[0] // 2
        upper = (member >> level) % 2
        keep = lax.dynamic_slice_in_dim(current, upper * size, size, 0)
        send = lax.dynamic_slice_in_dim(current, (1 - upper) * size, size, 0)
        current = keep + partner(send.astype(jnp.bfloat16), "dp", level).astype(send.dtype)
    stepped = (up_weight.astype(jnp.float32) - 0.002 * current).astype(jnp.bfloat16)
    levels = (lax.axis_size("dp") // 4).bit_length() - 1

    def make_branch(level):

        def branch(values):
            return jax.tree.map(
                lambda part, own: part.astype(own.dtype),
                shifted(shortened(values), "dp", 4 * 2**level),
                values,
            )

        return branch

    branches = [make_branch(level) for level in range(levels)]
    peer = lax.switch(step_index[0] % levels, branches, stepped)
    averaged_up = ((stepped.astype(jnp.float32) + peer.astype(jnp.float32)) * 0.5).astype(
        jnp.bfloat16
    )
    return (averaged_up, input_grad)


def solution(mesh):
    placed = (P("dp", "tensor"), P("dp", "tensor"), P("dp", "tensor"), P("dp", "tensor"), P())
    return jax.shard_map(
        shards,
        mesh=mesh,
        in_specs=placed,
        out_specs=(P("dp", "tensor"), P("dp", "tensor")),
        check_vma=False,
    )
```

profile of v0, /device:TPU:1, one launch (start us, length us, event | category | flops | bytes accessed | tf_op | source)
XLA Modules:
  0.0 284.3 jit_solution(10082720320704728868)
XLA Ops:
  7.2 0.0 all-gather.2.cloned.1.call-start
  7.2 8.8 %collective-permute-start.4 = (bf16[640,864]{0,1:T(8,128)(2,1)}, bf16[640,864]{0,1:T(8,128)(2,1)S(1)}, u32[]{:S(2)}, u32[]{:S(2)}) collective-permute-start(bf16[640,864]{0,1:T(8,128)(2,1)} %param.10), channel_id=1, source_target_pairs={{0,8},{8,0},{16,24},{24,16},{32,40},{40,32},{48,56},{56,48},{64,72... | collective-permute-start | bytes 3317768 | tf_op jit(solution)/shard_map/ppermute | solution.py:10
  16.0 1.9 collective-permute-start.8
  17.9 0.0 all-gather.2.cloned.1.call-update
  18.0 0.0 reduce-scatter.2.cloned.1.call-start
  18.0 0.0 copy-start.2
  18.0 0.5 collective-permute-done.4
  18.6 3.6 %maximum_select_fusion.2 = bf16[1280,864]{0,1:T(8,128)(2,1)} fusion(bf16[640,864]{0,1:T(8,128)(2,1)} %param.10, bf16[640,864]{0,1:T(8,128)(2,1)S(1)} %collective-permute-done.4, pred[]{:T(512)S(6)} %eq.14), kind=kLoop, calls=%fused_computation.6 | loop fusion | flops 9953280 | bytes 4423681 | tf_op jit(solution)/shard_map/jit(_where)/select_n | solution.py:23
  22.2 1.9 collective-permute-start.5
  24.1 0.0 collective-permute-done.8
  24.1 0.0 copy-done.2
  24.1 1.9 maximum_select_fusion.3
  26.0 3.4 %collective-permute-start.9 = (bf16[1280,864]{0,1:T(8,128)(2,1)}, bf16[1280,864]{0,1:T(8,128)(2,1)}, u32[]{:S(2)}, u32[]{:S(2)}) collective-permute-start(bf16[1280,864]{0,1:T(8,128)(2,1)} %maximum_select_fusion.3), channel_id=1, source_target_pairs={{0,16},{8,24},{16,0},{24,8},{32,48},{40,56},{48,32},{56,40},{64,80... | collective-permute-start | bytes 6635528 | tf_op jit(solution)/shard_map/ppermute | solution.py:10
  29.4 57.8 %all-gather.2.cloned.1.call-done = bf16[256,2560]{0,1:T(8,128)(2,1)} async-done(((bf16[256,320]{0,1:T(8,128)(2,1)}), bf16[256,2560]{0,1:T(8,128)(2,1)}) %all-gather.2.cloned.1.call-update) | async-done | bytes 1310736 | tf_op jit(solution)/shard_map/all_gather | solution.py:28
  87.2 0.0 copy-start.3
  87.2 0.0 collective-permute-done.5
  87.2 5.2 %convolution_bitcast_fusion.1 = f32[256,864]{0,1:T(8,128)S(1)} fusion(bf16[256,2560]{0,1:T(8,128)(2,1)} %all-gather.2.cloned.1.call-done, bf16[1280,864]{0,1:T(8,128)(2,1)} %maximum_select_fusion.2, bf16[1280,864]{0,1:T(8,128)(2,1)} %collective-permute-done.5, pred[]{:T(512)S(6)} %eq.13), kind=kOutput, calls=%fused_computation.15 | convolution fusion | flops 1152368640 | bytes 6619137 | tf_op jit(solution)/shard_map/dot_general | solution.py:35
  92.4 28.7 %collective-permute-done.9 = bf16[1280,864]{0,1:T(8,128)(2,1)} collective-permute-done((bf16[1280,864]{0,1:T(8,128)(2,1)}, bf16[1280,864]{0,1:T(8,128)(2,1)}, u32[]{:S(2)}, u32[]{:S(2)}) %collective-permute-start.9) | collective-permute-done | bytes 2211872 | tf_op jit(solution)/shard_map/ppermute | solution.py:10
  121.1 0.0 copy-done.3
  121.1 13.7 %fusion.7 = f32[256,2560]{0,1:T(8,128)} fusion(bf16[256,2560]{0,1:T(8,128)(2,1)S(1)} %copy-done.3, bf16[256,864]{0,1:T(8,128)(2,1)} %param.12, f32[256,864]{0,1:T(8,128)S(1)} %convolution_bitcast_fusion.1, bf16[1280,864]{0,1:T(8,128)(2,1)} %maximum_select_fusion.3, bf16[1280,864]{0,1:T(8,128)(2,1)} %collective-permute-done.9, pred[]{:T(512)S(6)} %eq.13, ...), kind=kOutput, calls=%fused_computation.21 | convolution fusion | flops 2307170304 | bytes 14106625 | tf_op jit(solution)/shard_map/dot_general | solution.py:44
  134.8 8.3 %convolution_add_fusion = f32[256,2560]{0,1:T(8,128)} fusion(f32[256,2560]{0,1:T(8,128)} %fusion.7, bf16[1280,864]{0,1:T(8,128)(2,1)} %maximum_select_fusion.3, bf16[1280,864]{0,1:T(8,128)(2,1)} %collective-permute-done.9, pred[]{:T(512)S(6)} %eq.13, f32[256,864]{0,1:T(8,128)S(1)} %convolution_bitcast_fusion.1, bf16[256,864]{0,1:T(8,128)(2,1)} %param.12), kind=kOutput, calls=%fused_computation.4 | convolution fusion | flops 1154572288 | bytes 10993665 | tf_op jit(solution)/shard_map/dot_general | solution.py:41
  143.1 0.0 reduce-scatter.2.cloned.1.call-update
  143.1 2.4 fusion.15
  145.5 0.0 copy-start
  145.5 3.4 %copy-done = f32[864,2560]{1,0:T(8,128)} copy-done((f32[864,2560]{1,0:T(8,128)}, f32[864,2560]{1,0:T(8,128)S(1)}, u32[]{:S(2)}) %copy-start) | copy-done | bytes 8847384
  149.0 1.6 fusion
  150.6 2.2 collective-permute-start.6
  152.8 48.3 %collective-permute-done.6 = bf16[1280,864]{0,1:T(8,128)(2,1)} collective-permute-done((bf16[1280,864]{0,1:T(8,128)(2,1)}, bf16[1280,864]{0,1:T(8,128)(2,1)}, u32[]{:S(2)}, u32[]{:S(2)}) %collective-permute-start.6) | collective-permute-done | bytes 2211872 | tf_op jit(solution)/shard_map/ppermute | solution.py:10
  201.2 3.4 %bitcast_add_fusion = f32[1280,864]{0,1:T(8,128)S(1)} fusion(bf16[1280,864]{0,1:T(8,128)(2,1)} %collective-permute-done.6, f32[864,2560]{1,0:T(8,128)} %copy-done, s32[]{:T(128)S(6)} %select_n.66), kind=kLoop, calls=%fused_computation.2 | loop fusion | flops 2211840 | bytes 11059204 | tf_op jit(solution)/shard_map/add | solution.py:58
  204.6 0.0 copy-start.1
  204.6 2.0 copy-done.1
  206.6 0.1 dynamic-slice_convert_fusion.1
  206.7 4.0 %collective-permute-start.7 = (bf16[640,864]{0,1:T(8,128)(2,1)S(1)}, bf16[640,864]{0,1:T(8,128)(2,1)S(1)}, u32[]{:S(2)}, u32[]{:S(2)}) collective-permute-start(bf16[640,864]{0,1:T(8,128)(2,1)S(1)} %dynamic-slice_convert_fusion.1), channel_id=1, source_target_pairs={{0,8},{8,0},{16,24},{24,16},{32,40},{40,32},{48,56},{56,48},{64,72... | collective-permute-start | bytes 3317768 | tf_op jit(solution)/shard_map/ppermute | solution.py:10
  211.4 1.7 collective-permute-done.7
  213.1 2.0 subtract_convert_fusion
  215.2 58.0 %conditional.4 = (bf16[640,864]{0,1:T(8,128)(2,1)}) conditional(s32[]{:T(128)} %clamp.3, bf16[640,864]{0,1:T(8,128)(2,1)S(1)} %subtract_convert_fusion, bf16[640,864]{0,1:T(8,128)(2,1)S(1)} %subtract_convert_fusion, bf16[640,864]{0,1:T(8,128)(2,1)S(1)} %subtract_convert_fusion, ...), branch_computations={%region_0.1_spmd, %region_1.2_spmd, %region_2.3_spmd, %region_3.4_... | conditional | bytes 4423728
  215.2 2.0 collective-permute-start.1
  217.2 56.0 %collective-permute-done.1 = bf16[640,864]{0,1:T(8,128)(2,1)} collective-permute-done((bf16[640,864]{0,1:T(8,128)(2,1)S(1)}, bf16[640,864]{0,1:T(8,128)(2,1)}, u32[]{:S(2)}, u32[]{:S(2)}) %collective-permute-start.1) | collective-permute-done | bytes 1105952 | tf_op jit(solution)/shard_map/cond/branch_1_fun/ppermute | solution.py:19
  273.2 2.6 multiply_convert_fusion
  275.8 0.0 reduce-scatter.2.cloned.1.call-done
  275.8 1.7 convert_element_type.77
Async XLA Ops:
  7.2 80.0 %all-gather.2.cloned.1.call-start = ((), (), s32[]{:S(2)}) async-start(), calls=%async_computation.1 | async-start | bytes 1474560 | tf_op jit(solution)/shard_map/all_gather | solution.py:28
  7.2 11.4 %collective-permute-start.4 = (bf16[640,864]{0,1:T(8,128)(2,1)}, bf16[640,864]{0,1:T(8,128)(2,1)S(1)}, u32[]{:S(2)}, u32[]{:S(2)}) collective-permute-start(bf16[640,864]{0,1:T(8,128)(2,1)} %param.10), channel_id=1, source_target_pairs={{0,8},{8,0},{16,24},{24,16},{32,40},{40,32},{48,56},{56,48},{64,72... | collective-permute-start | bytes 3317768 | tf_op jit(solution)/shard_map/ppermute | solution.py:10
  16.0 8.1 %collective-permute-start.8 = (bf16[640,864]{0,1:T(8,128)(2,1)}, bf16[640,864]{0,1:T(8,128)(2,1)S(1)}, u32[]{:S(2)}, u32[]{:S(2)}) collective-permute-start(bf16[640,864]{0,1:T(8,128)(2,1)} %param.11), channel_id=1, source_target_pairs={{0,8},{8,0},{16,24},{24,16},{32,40},{40,32},{48,56},{56,48},{64,72... | collective-permute-start | bytes 3317768 | tf_op jit(solution)/shard_map/ppermute | solution.py:10
  18.0 257.8 %reduce-scatter.2.cloned.1.call-start = ((), (), s32[]{:S(2)}) async-start(), calls=%async_computation.2 | async-start | bytes 2949120 | tf_op jit(solution)/shard_map/reduce_scatter | solution.py:47
  18.0 6.1 %copy-start.2 = (bf16[640,864]{0,1:T(8,128)(2,1)S(1)}, bf16[640,864]{0,1:T(8,128)(2,1)}, u32[]{:S(2)}) copy-start(bf16[640,864]{0,1:T(8,128)(2,1)} %param.11) | copy-start | bytes 3317764
  22.2 65.0 %collective-permute-start.5 = (bf16[1280,864]{0,1:T(8,128)(2,1)}, bf16[1280,864]{0,1:T(8,128)(2,1)}, u32[]{:S(2)}, u32[]{:S(2)}) collective-permute-start(bf16[1280,864]{0,1:T(8,128)(2,1)} %maximum_select_fusion.2), channel_id=1, source_target_pairs={{0,16},{8,24},{16,0},{24,8},{32,48},{40,56},{48,32},{56,40},{64,80... | collective-permute-start | bytes 6635528 | tf_op jit(solution)/shard_map/ppermute | solution.py:10
  26.0 95.1 %collective-permute-start.9 = (bf16[1280,864]{0,1:T(8,128)(2,1)}, bf16[1280,864]{0,1:T(8,128)(2,1)}, u32[]{:S(2)}, u32[]{:S(2)}) collective-permute-start(bf16[1280,864]{0,1:T(8,128)(2,1)} %maximum_select_fusion.3), channel_id=1, source_target_pairs={{0,16},{8,24},{16,0},{24,8},{32,48},{40,56},{48,32},{56,40},{64,80... | collective-permute-start | bytes 6635528 | tf_op jit(solution)/shard_map/ppermute | solution.py:10
  87.2 33.9 %copy-start.3 = (bf16[256,2560]{0,1:T(8,128)(2,1)S(1)}, bf16[256,2560]{0,1:T(8,128)(2,1)}, u32[]{:S(2)}) copy-start(bf16[256,2560]{0,1:T(8,128)(2,1)} %all-gather.2.cloned.1.call-done) | copy-start | bytes 3932164
  145.5 3.4 %copy-start = (f32[864,2560]{1,0:T(8,128)}, f32[864,2560]{1,0:T(8,128)S(1)}, u32[]{:S(2)}) copy-start(f32[864,2560]{1,0:T(8,128)S(1)} %fusion.15) | copy-start | bytes 26542084
  150.6 50.6 %collective-permute-start.6 = (bf16[1280,864]{0,1:T(8,128)(2,1)}, bf16[1280,864]{0,1:T(8,128)(2,1)}, u32[]{:S(2)}, u32[]{:S(2)}) collective-permute-start(bf16[1280,864]{0,1:T(8,128)(2,1)} %fusion), channel_id=1, source_target_pairs={{0,16},{8,24},{16,0},{24,8},{32,48},{40,56},{48,32},{56,40},{64,80... | collective-permute-start | bytes 6635528 | tf_op jit(solution)/shard_map/ppermute | solution.py:10
  204.6 2.0 copy-start.1
  206.7 6.4 %collective-permute-start.7 = (bf16[640,864]{0,1:T(8,128)(2,1)S(1)}, bf16[640,864]{0,1:T(8,128)(2,1)S(1)}, u32[]{:S(2)}, u32[]{:S(2)}) collective-permute-start(bf16[640,864]{0,1:T(8,128)(2,1)S(1)} %dynamic-slice_convert_fusion.1), channel_id=1, source_target_pairs={{0,8},{8,0},{16,24},{24,16},{32,40},{40,32},{48,56},{56,48},{64,72... | collective-permute-start | bytes 3317768 | tf_op jit(solution)/shard_map/ppermute | solution.py:10
  215.2 58.0 %collective-permute-start.1 = (bf16[640,864]{0,1:T(8,128)(2,1)S(1)}, bf16[640,864]{0,1:T(8,128)(2,1)}, u32[]{:S(2)}, u32[]{:S(2)}) collective-permute-start(bf16[640,864]{0,1:T(8,128)(2,1)S(1)} %param.1), channel_id=1, source_target_pairs={{0,64},{8,72},{16,80},{24,88},{32,96},{40,104},{48,112},{56,120},{... | collective-permute-start | bytes 3317768 | tf_op jit(solution)/shard_map/cond/branch_1_fun/ppermute | solution.py:19
Sparse Core Ops, SparseCore 0:
  18.1 69.0 all-gather.1
  143.3 111.7 reduce-scatter.1
where the time goes:
time: 285 us; the launch traced here: 284 us
  waiting for transfers between devices  193 us (68%)
  matrix products  29.6 us (10%)
  starting transfers between devices  24.3 us (9%)
  other arithmetic  15.2 us (5%)
  between operations  14.9 us (5%)
  local copies, waits for them, and re-layouts  7.2 us (3%)
    ppermute x6, waiting for transfers between devices, partner(): return lax.ppermute(value, axis, pairs)  79.2 us
    all_gather x1, waiting for transfers between devices, shards(): x_full = lax.all_gather(tokens, 'tensor', axis=1, tiled=True)  57.8 us
    ppermute x1, waiting for transfers between devices, shifted(): lax.ppermute(x, axis, [(i, (i + by) % devices) for i in range(devices)])  56 us
    ppermute x6, starting transfers between devices, partner(): return lax.ppermute(value, axis, pairs)  22.2 us
    dot_general x1, matrix products, shards(): lax.dot_general(gate_delta, gate_w, (((1,), (1,)), ((), ())), preferred_e...  13.7 us
    dot_general x1, matrix products, shards(): lax.dot_general(up_delta, up_w, (((1,), (1,)), ((), ())), preferred_eleme...  8.35 us
  transfers between devices with their start and end apart: 9, of which 6 were waited for; matrix products, arithmetic and copies ran while one was open for 8% of the time, Pallas kernels for 0%

commit v1 on v0

v1 whole, which is shorter than its diff:
```python
import functools

import jax
import jax.numpy as jnp
from jax import lax
from jax.experimental import pallas as pl
from jax.experimental.pallas import tpu as pltpu
from jax.sharding import PartitionSpec as P

MESH = pl.DeviceIdType.MESH
BF16, F32 = jnp.bfloat16, jnp.float32
WIDE = 256

X_Z, X_Y, X_FAR, X_NEAR = 0, 1, 3, 7
W_CORE, COT, X_CORE, PART, DELTA, STEP = 11, 13, 14, 15, 19, 23
G_NEAR, G_FAR, G_Y, G_Z, SENDS = 27, 31, 35, 37, 38
X_IN = 0
R_W, R_COT, R_XC, R_PART, R_DELTA, R_STEP = 9, 11, 12, 13, 17, 21
R_NEAR, R_FAR, R_Y, R_Z, RECVS = 25, 29, 33, 35, 36


def step_kernel(
    level, groups_dp, tok, gw, uw, cot, avg_ref, ig_ref,
    xin, xr, xs, xt, wgb, wub, hg,
    pf_m, pf_t, sb_m, sb_t, rb_m, rb_t, ud_m, ud_t, us_m, us_t, gd_m, gd_t,
    st_m, st_t, pr_m, pr_t, acc, near_out, near_in, far_out, far_in, y_out, y_in, z_out, z_in,
    avg_buf, ig_buf, snd, rcv, loc,
):
    T, F = tok.shape
    R, C = gw.shape
    full = C // WIDE
    rest = C - full * WIDE
    dp, t = lax.axis_index("dp"), lax.axis_index("tensor")
    core, side = lax.rem(dp, 2), lax.rem(dp // 2, 2)
    x, zh = t // 2, lax.rem(t, 2)
    place = lax.rem(x - 2 * side + 4, 4)
    home = place < 2
    away = place >= 2
    odd = lax.rem(place, 2)
    prim = jnp.where(home, odd, 1 - odd)
    xbit = lax.rem(x, 2)

    sibling = (dp + 1 - 2 * core, t)
    across = (dp + 2 - 4 * side, t)
    anti = (dp, t + 1 - 2 * zh)
    near = (dp, (x + 1 - 2 * xbit) * 2 + zh)
    far = (dp, lax.rem(2 * side + 3 - place, 4) * 2 + zh)
    shift = 4 * 2**level
    target = (lax.rem(dp + shift, groups_dp), t)
    origin = (lax.rem(dp + groups_dp - shift, groups_dp), t)

    partners = [sibling, across, anti, near, far, target]
    if 2 * shift != groups_dp:
        partners.append(origin)
    barrier = pltpu.get_barrier_semaphore()
    for partner in partners:
        pl.semaphore_signal(barrier, inc=1, device_id=partner, device_id_type=MESH)
    pl.semaphore_wait(barrier, len(partners))

    def remote(src, dst, s, r, device):
        return pltpu.make_async_remote_copy(
            src_ref=src, dst_ref=dst, send_sem=snd.at[s], recv_sem=rcv.at[r],
            device_id=device, device_id_type=MESH,
        )

    def slot(i, z, y):
        return (i * 2 + z) * 2 + y

    blocks = [(zh, side), (zh, 1 - side), (1 - zh, side), (1 - zh, 1 - side)]

    def to_x(n, src, which, device):
        index = slot(prim, *blocks[n])
        return remote(src, xin.at[index], which + n, X_IN + index, device)

    def arrived(index):
        remote(tok, xin.at[index], X_Z, X_IN + index, anti).wait_recv()

    z_slot = jnp.where(home, slot(xbit, zh, side), 8)
    z_in_slot = jnp.where(home, slot(xbit, 1 - zh, side), 8)
    z_copy = remote(tok, xin.at[z_slot], X_Z, X_IN + z_slot, anti)
    y_first, y_second = slot(xbit, zh, side), slot(xbit, 1 - zh, side)
    y_own = remote(tok, xin.at[y_first], X_Y, X_IN + y_first, across)
    y_anti = remote(xin.at[8], xin.at[y_second], X_Y + 1, X_IN + y_second, across)
    own_x = pltpu.make_async_copy(tok, xin.at[slot(xbit, zh, side)], loc.at[0])
    cot_copy = remote(cot, hg.at[side], COT, R_COT, across)
    z_copy.start()

    @pl.when(home)
    def _():
        own_x.start()
        to_x(0, tok, X_FAR, far).start()
        to_x(0, tok, X_NEAR, near).start()
        cot_copy.start()

    @pl.when(away)
    def _():
        y_own.start()

    w_copies = [
        remote(gw, wgb.at[core], W_CORE, R_W, sibling),
        remote(uw, wub.at[core], W_CORE + 1, R_W + 1, sibling),
    ]
    own_copies = [
        pltpu.make_async_copy(gw, wgb.at[core], loc.at[1]),
        pltpu.make_async_copy(uw, wub.at[core], loc.at[2]),
        pltpu.make_async_copy(cot, hg.at[side], loc.at[3]),
    ]
    for copy in own_copies + w_copies:
        copy.start()

    @pl.when(home)
    def _():
        for n in (1, 2, 3):
            index = slot(prim, *blocks[n])
            arrived(index)
            to_x(n, xin.at[index], X_FAR, far).start()
            to_x(n, xin.at[index], X_NEAR, near).start()
        own_x.wait()

    @pl.when(away)
    def _():
        for n in range(4):
            if n == 1:
                arrived(z_in_slot)
                y_anti.start()
                cot_copy.start()
            index = slot(prim, *blocks[n])
            arrived(index)
            to_x(n, xin.at[index], X_FAR, near).start()

    acc[...] = jnp.zeros_like(acc)
    for n in range(4):
        arrived(slot(1 - prim, *blocks[n]))
    for i in range(2):
        for y in range(2):
            xr[i, y * T : (y + 1) * T, :] = jnp.concatenate(
                [xin[slot(i, 0, y)], xin[slot(i, 1, y)]], axis=1
            )
    x_copy = remote(xr.at[1 - core], xs, X_CORE, R_XC, sibling)
    x_copy.start()
    for copy in own_copies:
        copy.wait()
    for copy in w_copies:
        copy.wait_recv()

    class Part:
        def __init__(self, j, main):
            pick = (lambda a, b: a.at[j]) if main else (lambda a, b: b)
            self.width = WIDE if main else rest
            start = pl.multiple_of(j * WIDE, WIDE) if main else full * WIDE
            self.columns = pl.ds(start, self.width)
            self.pf, self.sb, self.rb = pick(pf_m, pf_t), pick(sb_m, sb_t), pick(rb_m, rb_t)
            self.ud, self.us, self.gd = pick(ud_m, ud_t), pick(us_m, us_t), pick(gd_m, gd_t)
            self.st, self.pr = pick(st_m, st_t), pick(pr_m, pr_t)
            self.j = j

        def sums(self):
            return remote(self.sb, self.rb, PART + self.j, R_PART + self.j, across)

        def deltas(self):
            return remote(self.ud, self.us, DELTA + self.j, R_DELTA + self.j, sibling)

        def peer(self):
            return remote(self.st, self.pr, STEP + self.j, R_STEP + self.j, target)

    def each_part(body):
        @pl.loop(0, full)
        def _(j):
            body(Part(j, True))

        if rest:
            body(Part(full, False))

    def rows_of(r, size):
        return pl.ds(pl.multiple_of(r * size, size), size)

    def sums(part):
        @pl.loop(0, 2)
        def _(r):
            rows = rows_of(r, T)
            for n, w in ((0, wgb), (1, wub)):
                total = jnp.dot(
                    xr[0, rows, :], w[0, :, part.columns], preferred_element_type=F32
                ) + jnp.dot(xr[1, rows, :], w[1, :, part.columns], preferred_element_type=F32)
                part.pf[n, rows, :] = total
                part.sb[n, rows, :] = total.astype(BF16)

        part.sums().start()

    each_part(sums)

    xt[:, : 2 * T] = xr[core].T
    x_copy.wait_recv()
    xt[:, 2 * T :] = xs[...].T
    cot_copy.wait_recv()

    tile = 64 if T % 64 == 0 else T

    def deltas(part):
        part.sums().wait_recv()
        for y in range(2):

            @pl.loop(0, T // tile)
            def _(r):
                rows = pl.ds(pl.multiple_of(y * T + r * tile, tile), tile)
                gate = part.pf[0, rows, :] + part.rb[0, rows, :].astype(F32)
                up = part.pf[1, rows, :] + part.rb[1, rows, :].astype(F32)
                sig = 1.0 / (1.0 + jnp.exp(-gate))
                wide = hg[y, rows_of(r, tile), part.columns].astype(F32)
                part.ud[rows, :] = (wide * gate * sig).astype(BF16)
                part.gd[rows, :] = (wide * up * sig * (1.0 + gate * (1.0 - sig))).astype(BF16)

        part.deltas().start()

        @pl.loop(0, 2)
        def _(r):
            rows = rows_of(r, T)
            for i in range(2):
                acc[i, rows, :] += lax.dot_general(
                    part.ud[rows, :], wub[i, :, part.columns], (((1,), (1,)), ((), ())),
                    preferred_element_type=F32,
                ) + lax.dot_general(
                    part.gd[rows, :], wgb[i, :, part.columns], (((1,), (1,)), ((), ())),
                    preferred_element_type=F32,
                )

        part.deltas().wait_recv()

        @pl.loop(0, R // 128)
        def _(r):
            rows = rows_of(r, 128)
            grad = jnp.dot(xt[rows, : 2 * T], part.ud[...], preferred_element_type=F32) + jnp.dot(
                xt[rows, 2 * T :], part.us[...], preferred_element_type=F32
            )
            old = wub[core, rows, part.columns].astype(F32)
            part.st[rows, :] = (old - 0.002 * grad).astype(BF16)

        part.peer().start()

    each_part(deltas)

    H = T // 2
    pieces = [(1 - side, 0), (1 - side, 1), (side, 0), (side, 1)]

    def piece_rows(n):
        y, half = pieces[n]
        return pl.ds(pl.multiple_of(y * T + half * H, H), H)

    def g_near(n):
        return remote(near_out.at[n], near_in.at[n], G_NEAR + n, R_NEAR + n, near)

    def g_far(n):
        return remote(far_out.at[n], far_in.at[n], G_FAR + n, R_FAR + n, far)

    def g_y(half):
        return remote(y_out.at[half], y_in.at[half], G_Y + half, R_Y + half, across)

    for n in range(4):
        near_out[n] = acc[1 - prim, piece_rows(n), :].astype(BF16)
        g_near(n).start()

    @pl.when(away)
    def _():
        for n in range(4):
            g_near(n).wait_recv()
            far_out[n] = (
                acc[prim, piece_rows(n), :] + near_in[n].astype(F32)
            ).astype(BF16)
            g_far(n).start()

    def at_home(n):
        g_near(n).wait_recv()
        g_far(n).wait_recv()
        return (
            acc[prim, piece_rows(n), :] + near_in[n].astype(F32) + far_in[n].astype(F32)
        )

    mine = acc.at[prim]
    own = pl.ds(pl.multiple_of(side * T, T), T)

    @pl.when(home)
    def _():
        for n in range(2):
            y_out[n] = at_home(n).astype(BF16)
            g_y(n).start()
        for n in range(2, 4):
            mine[piece_rows(n), :] = at_home(n)

    @pl.when(away)
    def _():
        for n in range(2):
            g_y(n).wait_recv()
            mine[piece_rows(n + 2), :] = y_in[n].astype(F32)

    total = mine[own, :]
    low, high = total[:, :F], total[:, F:]
    z_out[...] = jnp.where(zh == 0, high, low).astype(BF16)
    g_z = remote(z_out, z_in, G_Z, R_Z, anti)
    g_z.start()
    g_z.wait_recv()
    ig_buf[...] = (jnp.where(zh == 0, low, high) + z_in[...].astype(F32)).astype(BF16)
    ig_copy = pltpu.make_async_copy(ig_buf, ig_ref, loc.at[4])
    ig_copy.start()

    def average(part):
        part.peer().wait_recv()
        avg_buf[:, part.columns] = (
            (part.st[...].astype(F32) + part.pr[...].astype(F32)) * 0.5
        ).astype(BF16)

    each_part(average)
    avg_copy = pltpu.make_async_copy(avg_buf, avg_ref, loc.at[5])
    avg_copy.start()

    z_copy.wait_send()
    cot_copy.wait_send()
    x_copy.wait_send()
    for copy in w_copies:
        copy.wait_send()
    for n in range(4):
        to_x(n, tok, X_FAR, far).wait_send()
        g_near(n).wait_send()

    @pl.when(home)
    def _():
        for n in range(4):
            to_x(n, tok, X_NEAR, near).wait_send()
        for n in range(2):
            g_y(n).wait_send()

    @pl.when(away)
    def _():
        y_own.wait_send()
        y_anti.wait_send()
        for n in range(4):
            g_far(n).wait_send()

    def left(part):
        part.sums().wait_send()
        part.deltas().wait_send()
        part.peer().wait_send()

    each_part(left)
    g_z.wait_send()
    ig_copy.wait()
    avg_copy.wait()


def call_step(level, groups_dp, tokens, gate_weight, up_weight, hidden_grad):
    T, F = tokens.shape
    R, C = gate_weight.shape
    full = C // WIDE
    rest = C - full * WIDE

    def both(shape, kind):
        return [
            pltpu.VMEM((full, *shape, WIDE), kind),
            pltpu.VMEM((*shape, rest), kind),
        ]

    scratch = [
        pltpu.VMEM((9, T, F), BF16),
        pltpu.VMEM((2, 2 * T, R), BF16),
        pltpu.VMEM((2 * T, R), BF16),
        pltpu.VMEM((R, 4 * T), BF16),
        pltpu.VMEM((2, R, C), BF16),
        pltpu.VMEM((2, R, C), BF16),
        pltpu.VMEM((2, T, C), BF16),
        *both((2, 2 * T), F32),
        *both((2, 2 * T), BF16),
        *both((2, 2 * T), BF16),
        *both((2 * T,), BF16),
        *both((2 * T,), BF16),
        *both((2 * T,), BF16),
        *both((R,), BF16),
        *both((R,), BF16),
        pltpu.VMEM((2, 2 * T, R), F32),
        pltpu.VMEM((4, T // 2, R), BF16),
        pltpu.VMEM((4, T // 2, R), BF16),
        pltpu.VMEM((4, T // 2, R), BF16),
        pltpu.VMEM((4, T // 2, R), BF16),
        pltpu.VMEM((2, T // 2, R), BF16),
        pltpu.VMEM((2, T // 2, R), BF16),
        pltpu.VMEM((T, F), BF16),
        pltpu.VMEM((T, F), BF16),
        pltpu.VMEM((R, C), BF16),
        pltpu.VMEM((T, F), BF16),
        pltpu.SemaphoreType.DMA((SENDS,)),
        pltpu.SemaphoreType.DMA((RECVS,)),
        pltpu.SemaphoreType.DMA((6,)),
    ]
    return pl.pallas_call(
        functools.partial(step_kernel, level, groups_dp),
        out_shape=(
            jax.ShapeDtypeStruct((R, C), BF16),
            jax.ShapeDtypeStruct((T, F), BF16),
        ),
        in_specs=[pl.BlockSpec(memory_space=pl.ANY)] * 4,
        out_specs=[pl.BlockSpec(memory_space=pl.ANY)] * 2,
        scratch_shapes=scratch,
        compiler_params=pltpu.CompilerParams(
            collective_id=level, has_side_effects=True, vmem_limit_bytes=56 * 2**20
        ),
        cost_estimate=pl.CostEstimate(
            flops=20 * T * 8 * F * C, bytes_accessed=6 * R * C, transcendentals=2 * T * C
        ),
    )(tokens, gate_weight, up_weight, hidden_grad)


def shards(tokens, gate_weight, up_weight, hidden_grad, step_index):
    devices = lax.axis_size("dp")
    levels = (devices // 4).bit_length() - 1
    branches = [functools.partial(call_step, level, devices) for level in range(levels)]
    return lax.switch(
        step_index[0] % levels, branches, tokens, gate_weight, up_weight, hidden_grad
    )


def solution(mesh):
    placed = (P("dp", "tensor"), P("dp", "tensor"), P("dp", "tensor"), P("dp", "tensor"), P())
    return jax.shard_map(
        shards,
        mesh=mesh,
        in_specs=placed,
        out_specs=(P("dp", "tensor"), P("dp", "tensor")),
        check_vma=False,
    )
```

time: 285 us -> 153 us (0.54)
  the two profiles are of different devices: /device:TPU:1 before, /device:TPU:8 now
where the time goes in v1:
time: 153 us
  Pallas kernels  141 us (92%)
  local copies, waits for them, and re-layouts  10.5 us (7%)
    pallas_call x1, Pallas kernels, call_step(): pl.pallas_call(functools.partial(step_kernel, level, groups_dp), out_shap...  141 us
    another operation x4, local copies, waits for them, and re-layouts  7.31 us
    cond x2, local copies, waits for them, and re-layouts, shards(): lax.switch(step_index[0] % levels, branches, tokens, gate_weight, up_weig...  3.2 us

profile of v1, /device:TPU:8, one launch (start us, length us, event | category | flops | bytes accessed | tf_op | source)
XLA Modules:
  0.0 152.8 jit_solution(6309919697809550608)
XLA Ops:
  1.3 151.5 %conditional.1 = (bf16[640,864]{0,1:T(8,128)(2,1)}, bf16[256,320]{0,1:T(8,128)(2,1)}) conditional(s32[]{:T(128)} %clamp.3, (bf16[256,320]{0,1:T(8,128)(2,1)}, bf16[640,864]{0,1:T(8,128)(2,1)}, bf16[640,864]{0,1:T(8,128)(2,1)}, bf16[256,864]{0,1:T(8,128)(2,1)}) %tuple.19, (bf16[256,320]{0,1:T(8,128)(2,1)}, ...), branch_computations={%region_0.1_spmd, %region_1.2_spmd, %region_2.3_spmd, %region_3.4_... | conditional | flops 11324620800 | bytes 20996196 | solution.py:414
  1.3 0.0 copy-start.4
  1.3 1.8 %copy.15.tok = bf16[256,320]{1,0:T(8,128)(2,1)} copy(bf16[256,320]{0,1:T(8,128)(2,1)} %get-tuple-element.60) | data formatting | bytes 327680 | tf_op jit(solution)/shard_map
  3.1 2.0 %copy.18.cot = bf16[256,864]{1,0:T(8,128)(2,1)} copy(bf16[256,864]{0,1:T(8,128)(2,1)} %get-tuple-element.63) | data formatting | bytes 884736 | tf_op jit(solution)/shard_map
  5.1 0.0 copy-done.4
  5.1 0.0 copy-start
  5.1 1.8 %copy.17.uw = bf16[640,864]{1,0:T(8,128)(2,1)} copy(bf16[640,864]{0,1:T(8,128)(2,1)S(1)} %copy-done.4) | data formatting | bytes 2211840 | tf_op jit(solution)/shard_map
  6.9 0.0 copy-done
  6.9 1.8 %copy.16.gw = bf16[640,864]{1,0:T(8,128)(2,1)} copy(bf16[640,864]{0,1:T(8,128)(2,1)S(1)} %copy-done) | data formatting | bytes 2211840 | tf_op jit(solution)/shard_map
  8.6 140.9 %branch_0_fun.1 = (bf16[640,864]{1,0:T(8,128)(2,1)}, bf16[256,320]{1,0:T(8,128)(2,1)}) custom-call(bf16[256,320]{1,0:T(8,128)(2,1)} %copy.15.tok, bf16[640,864]{1,0:T(8,128)(2,1)} %copy.16.gw, bf16[640,864]{1,0:T(8,128)(2,1)} %copy.17.uw, bf16[256,864]{1,0:T(8,128)(2,1)} %copy.18.cot), custom_call_target="tpu_custom_call" | custom-call | flops 11324620800 | bytes 3317760 | tf_op jit(solution)/shard_map/cond/branch_0_fun/pallas_call | solution.py:392
  149.6 0.0 copy-start.8
  149.6 2.4 %copy.33 = bf16[640,864]{0,1:T(8,128)(2,1)} copy(bf16[640,864]{1,0:T(8,128)(2,1)} %get-tuple-element.78) | data formatting | bytes 2211840 | tf_op jit(solution)/shard_map/cond | solution.py:414
  152.0 0.0 copy-done.8
  152.0 0.8 copy.37
Async XLA Ops:
  1.3 3.8 %copy-start.4 = (bf16[640,864]{0,1:T(8,128)(2,1)S(1)}, bf16[640,864]{0,1:T(8,128)(2,1)}, u32[]{:S(2)}) copy-start(bf16[640,864]{0,1:T(8,128)(2,1)} %get-tuple-element.62) | copy-start | bytes 3317764 | tf_op jit(solution)/shard_map/cond
  5.1 1.8 %copy-start = (bf16[640,864]{0,1:T(8,128)(2,1)S(1)}, bf16[640,864]{0,1:T(8,128)(2,1)}, u32[]{:S(2)}) copy-start(bf16[640,864]{0,1:T(8,128)(2,1)} %get-tuple-element.61) | copy-start | bytes 3317764 | tf_op jit(solution)/shard_map/cond
  149.6 2.4 %copy-start.8 = (bf16[256,320]{1,0:T(8,128)(2,1)S(1)}, bf16[256,320]{1,0:T(8,128)(2,1)}, u32[]{:S(2)}) copy-start(bf16[256,320]{1,0:T(8,128)(2,1)} %get-tuple-element.79) | copy-start | bytes 491524 | tf_op jit(solution)/shard_map/cond

commit v2 on v0

v2 whole, which is shorter than its diff:
```python
import functools

import jax
import jax.numpy as jnp
from jax import lax
from jax.experimental import pallas as pl
from jax.experimental.pallas import tpu as pltpu
from jax.sharding import PartitionSpec as P

MESH = pl.DeviceIdType.MESH
BF16, F32 = jnp.bfloat16, jnp.float32
PARTS = 3

X_Z, X_Y, X_FAR, X_NEAR = 0, 1, 3, 7
W_CORE, COT, X_CORE, PART, DELTA, STEP = 11, 13, 14, 15, 15 + PARTS, 15 + 2 * PARTS
G_NEAR = 15 + 3 * PARTS
G_FAR, G_Y, G_Z, SENDS = G_NEAR + 4, G_NEAR + 8, G_NEAR + 10, G_NEAR + 11
R_X, R_W, R_COT, R_XC, R_PART, R_DELTA, R_STEP = 0, 9, 11, 12, 13, 13 + PARTS, 13 + 2 * PARTS
R_NEAR = 13 + 3 * PARTS
R_FAR, R_Y, R_Z, RECVS = R_NEAR + 4, R_NEAR + 8, R_NEAR + 10, R_NEAR + 11


def step_kernel(
    level, groups_dp, tok, gw, uw, cot, avg_ref, ig_ref,
    xin, xz, xs, xt, wgb, wub, wgt, wut, hg, pf, sb, rb, ud, us, gd, st, pr,
    acc, near_out, near_in, far_out, far_in, y_out, y_in, z_out, z_in,
    ig_buf, snd, rcv, loc,
):
    F, T = tok.shape
    C, R = gw.shape
    n_part = C // PARTS
    dp, t = lax.axis_index("dp"), lax.axis_index("tensor")
    core, side = lax.rem(dp, 2), lax.rem(dp // 2, 2)
    x, zh = t // 2, lax.rem(t, 2)
    place = lax.rem(x - 2 * side + 4, 4)
    home = place < 2
    away = place >= 2
    odd = lax.rem(place, 2)
    prim = jnp.where(home, odd, 1 - odd)
    xbit = lax.rem(x, 2)

    sibling = (dp + 1 - 2 * core, t)
    across = (dp + 2 - 4 * side, t)
    anti = (dp, t + 1 - 2 * zh)
    near = (dp, (x + 1 - 2 * xbit) * 2 + zh)
    far = (dp, lax.rem(2 * side + 3 - place, 4) * 2 + zh)
    shift = 4 * 2**level
    target = (lax.rem(dp + shift, groups_dp), t)
    origin = (lax.rem(dp + groups_dp - shift, groups_dp), t)

    partners = [sibling, across, anti, near, far, target]
    if 2 * shift != groups_dp:
        partners.append(origin)
    barrier = pltpu.get_barrier_semaphore()
    for partner in partners:
        pl.semaphore_signal(barrier, inc=1, device_id=partner, device_id_type=MESH)
    pl.semaphore_wait(barrier, len(partners))

    drain = []

    def remote(src, dst, s, r, device):
        return pltpu.make_async_remote_copy(
            src_ref=src, dst_ref=dst, send_sem=snd.at[s], recv_sem=rcv.at[r],
            device_id=device, device_id_type=MESH,
        )

    def rows_of(r, size):
        return pl.ds(pl.multiple_of(r * size, size), size)

    def block_of(ref, i, z, y):
        return ref.at[i, rows_of(z, F), rows_of(y, T)]

    def slot(i, z, y):
        return (i * 2 + z) * 2 + y

    blocks = [(zh, side), (zh, 1 - side), (1 - zh, side), (1 - zh, 1 - side)]

    def to_x(n, src, which, device):
        where = (prim, *blocks[n])
        src = block_of(xin, *where) if src is None else src
        return remote(src, block_of(xin, *where), which + n, R_X + slot(*where), device)

    def x_arrived(i, n):
        where = (i, *blocks[n])
        remote(tok, block_of(xin, *where), X_Z, R_X + slot(*where), anti).wait_recv()

    mine = (xbit, zh, side)
    later = (xbit, 1 - zh, side)
    z_home = remote(tok, block_of(xin, *mine), X_Z, R_X + slot(*mine), anti)
    z_away = remote(tok, xz, X_Z, R_X + 8, anti)
    y_own = remote(tok, block_of(xin, *mine), X_Y, R_X + slot(*mine), across)
    y_anti = remote(xz, block_of(xin, *later), X_Y + 1, R_X + slot(*later), across)
    own_x = pltpu.make_async_copy(tok, block_of(xin, *mine), loc.at[0])
    cot_copy = remote(cot, hg.at[:, rows_of(side, T)], COT, R_COT, across)

    @pl.when(home)
    def _():
        z_home.start()
        to_x(0, tok, X_FAR, far).start()
        to_x(0, tok, X_NEAR, near).start()
        own_x.start()
        cot_copy.start()

    @pl.when(away)
    def _():
        z_away.start()
        y_own.start()

    w_copies = [
        remote(gw, wgb.at[core], W_CORE, R_W, sibling),
        remote(uw, wub.at[core], W_CORE + 1, R_W + 1, sibling),
    ]
    own_copies = [
        pltpu.make_async_copy(gw, wgb.at[core], loc.at[1]),
        pltpu.make_async_copy(uw, wub.at[core], loc.at[2]),
        pltpu.make_async_copy(cot, hg.at[:, rows_of(side, T)], loc.at[3]),
    ]
    for copy in own_copies + w_copies:
        copy.start()

    @pl.when(home)
    def _():
        for n in (1, 2, 3):
            x_arrived(prim, n)
            to_x(n, None, X_FAR, far).start()
            to_x(n, None, X_NEAR, near).start()
        own_x.wait()

    @pl.when(away)
    def _():
        for n in range(4):
            if n == 1:
                z_away.wait_recv()
                y_anti.start()
                cot_copy.start()
            x_arrived(prim, n)
            to_x(n, None, X_FAR, near).start()

    for copy in own_copies:
        copy.wait()
    for copy in w_copies:
        copy.wait_recv()
    for n in range(4):
        x_arrived(1 - prim, n)

    def x_left():
        z_home.wait_send()
        cot_copy.wait_send()
        for copy in w_copies:
            copy.wait_send()
        for n in range(4):
            to_x(n, tok, X_FAR, far).wait_send()

        @pl.when(home)
        def _():
            for n in range(4):
                to_x(n, tok, X_NEAR, near).wait_send()

        @pl.when(away)
        def _():
            y_own.wait_send()
            y_anti.wait_send()

    drain.append(x_left)

    x_copy = remote(xin.at[1 - core], xs, X_CORE, R_XC, sibling)
    x_copy.start()
    drain.append(lambda: x_copy.wait_send())

    def sums_copy(j):
        return remote(sb.at[j], rb.at[j], PART + j, R_PART + j, across)

    def delta_copy(j):
        return remote(ud.at[j], us.at[j], DELTA + j, R_DELTA + j, sibling)

    def step_copy(j):
        return remote(st.at[rows_of(j, n_part)], pr.at[rows_of(j, n_part)], STEP + j, R_STEP + j, target)

    def parts_left(which):
        @pl.loop(0, PARTS)
        def _(j):
            which(j).wait_send()

    @pl.loop(0, PARTS)
    def _(j):
        rows = rows_of(j, n_part)
        for n, w in ((0, wgb), (1, wub)):
            total = jnp.dot(w[0, rows, :], xin[0], preferred_element_type=F32) + jnp.dot(
                w[1, rows, :], xin[1], preferred_element_type=F32
            )
            pf[j, n] = total
            sb[j, n] = total.astype(BF16)
        sums_copy(j).start()

    drain.append(lambda: parts_left(sums_copy))

    @pl.loop(0, PARTS)
    def _(j):
        rows = rows_of(j, n_part)
        for i in range(2):
            wgt[j, i] = wgb[i, rows, :].T
            wut[j, i] = wub[i, rows, :].T

    acc[...] = jnp.zeros_like(acc)
    xt[: 2 * T, :] = xin[core].T
    x_copy.wait_recv()
    xt[2 * T :, :] = xs[...].T
    cot_copy.wait_recv()

    @pl.loop(0, PARTS)
    def _(j):
        sums_copy(j).wait_recv()
        tile = 32 if n_part % 32 == 0 else 16

        @pl.loop(0, n_part // tile)
        def _(r):
            rows = rows_of(r, tile)
            gate = pf[j, 0, rows, :] + rb[j, 0, rows, :].astype(F32)
            up = pf[j, 1, rows, :] + rb[j, 1, rows, :].astype(F32)
            sig = 1.0 / (1.0 + jnp.exp(-gate))
            at = pl.ds(pl.multiple_of(j * n_part + r * tile, tile), tile)
            wide = hg[at, :].astype(F32)
            ud[j, rows, :] = (wide * gate * sig).astype(BF16)
            gd[j, rows, :] = (wide * up * sig * (1.0 + gate * (1.0 - sig))).astype(BF16)

        delta_copy(j).start()

        for i in range(2):
            @pl.loop(0, 2)
            def _(r):
                rows = rows_of(r, R // 2)
                acc[i, rows, :] += jnp.dot(
                    wut[j, i, rows, :], ud[j], preferred_element_type=F32
                ) + jnp.dot(wgt[j, i, rows, :], gd[j], preferred_element_type=F32)

        delta_copy(j).wait_recv()
        grad = jnp.dot(ud[j], xt[: 2 * T, :], preferred_element_type=F32) + jnp.dot(
            us[j], xt[2 * T :, :], preferred_element_type=F32
        )
        rows = rows_of(j, n_part)
        st[rows, :] = (wub[core, rows, :].astype(F32) - 0.002 * grad).astype(BF16)
        step_copy(j).start()

    drain.append(lambda: parts_left(delta_copy))
    drain.append(lambda: parts_left(step_copy))

    pieces = [(1 - zh, 1 - side), (zh, 1 - side), (1 - zh, side), (zh, side)]

    def piece(i, n):
        return block_of(acc, i, *pieces[n])

    def g_near(n):
        return remote(near_out.at[n], near_in.at[n], G_NEAR + n, R_NEAR + n, near)

    def g_far(n):
        return remote(far_out.at[n], far_in.at[n], G_FAR + n, R_FAR + n, far)

    def g_y(n):
        return remote(y_out.at[n], y_in.at[n], G_Y + n, R_Y + n, across)

    def g_z(src):
        return remote(src, z_in, G_Z, R_Z, anti)

    for n in range(4):
        near_out[n] = piece(1 - prim, n)[...].astype(BF16)
        g_near(n).start()

    @pl.when(away)
    def _():
        for n in range(4):
            g_near(n).wait_recv()
            far_out[n] = (piece(prim, n)[...] + near_in[n].astype(F32)).astype(BF16)
            g_far(n).start()
        g_y(0).wait_recv()
        g_z(y_in.at[0]).start()
        g_y(1).wait_recv()
        g_z(z_out).wait_recv()
        ig_buf[...] = (y_in[1].astype(F32) + z_in[...].astype(F32)).astype(BF16)

    @pl.when(home)
    def _():
        def total(n):
            g_near(n).wait_recv()
            g_far(n).wait_recv()
            return piece(prim, n)[...] + near_in[n].astype(F32) + far_in[n].astype(F32)

        for n in range(2):
            y_out[n] = total(n).astype(BF16)
            g_y(n).start()
        z_out[...] = total(2).astype(BF16)
        g_z(z_out).start()
        last = total(3)
        g_z(z_out).wait_recv()
        ig_buf[...] = (last + z_in[...].astype(F32)).astype(BF16)

    ig_copy = pltpu.make_async_copy(ig_buf, ig_ref, loc.at[4])
    ig_copy.start()

    def ig_left():
        ig_copy.wait()
        for n in range(4):
            g_near(n).wait_send()
        g_z(z_out).wait_send()

        @pl.when(home)
        def _():
            for n in range(2):
                g_y(n).wait_send()

        @pl.when(away)
        def _():
            for n in range(4):
                g_far(n).wait_send()

    drain.append(ig_left)

    @pl.loop(0, PARTS)
    def _(j):
        rows = rows_of(j, n_part)
        step_copy(j).wait_recv()
        step_copy(j).wait_send()
        st[rows, :] = (
            (st[rows, :].astype(F32) + pr[rows, :].astype(F32)) * 0.5
        ).astype(BF16)
        pltpu.make_async_copy(st.at[rows], avg_ref.at[rows], loc.at[5 + j]).start()

    drain.pop(-2)

    @pl.loop(0, PARTS)
    def _(j):
        rows = rows_of(j, n_part)
        pltpu.make_async_copy(st.at[rows], avg_ref.at[rows], loc.at[5 + j]).wait()

    for left in drain:
        left()


def call_step(level, groups_dp, tokens, gate_weight, up_weight, hidden_grad):
    F, T = tokens.shape
    C, R = gate_weight.shape
    n_part = C // PARTS
    vmem = pltpu.VMEM
    scratch = [
        vmem((2, R, 2 * T), BF16),
        vmem((F, T), BF16),
        vmem((R, 2 * T), BF16),
        vmem((4 * T, R), BF16),
        vmem((2, C, R), BF16),
        vmem((2, C, R), BF16),
        vmem((PARTS, 2, R, n_part), BF16),
        vmem((PARTS, 2, R, n_part), BF16),
        vmem((C, 2 * T), BF16),
        vmem((PARTS, 2, n_part, 2 * T), F32),
        vmem((PARTS, 2, n_part, 2 * T), BF16),
        vmem((PARTS, 2, n_part, 2 * T), BF16),
        vmem((PARTS, n_part, 2 * T), BF16),
        vmem((PARTS, n_part, 2 * T), BF16),
        vmem((PARTS, n_part, 2 * T), BF16),
        vmem((C, R), BF16),
        vmem((C, R), BF16),
        vmem((2, R, 2 * T), F32),
        vmem((4, F, T), BF16),
        vmem((4, F, T), BF16),
        vmem((4, F, T), BF16),
        vmem((4, F, T), BF16),
        vmem((2, F, T), BF16),
        vmem((2, F, T), BF16),
        vmem((F, T), BF16),
        vmem((F, T), BF16),
        vmem((F, T), BF16),
        pltpu.SemaphoreType.DMA((SENDS,)),
        pltpu.SemaphoreType.DMA((RECVS,)),
        pltpu.SemaphoreType.DMA((5 + PARTS,)),
    ]
    return pl.pallas_call(
        functools.partial(step_kernel, level, groups_dp),
        out_shape=(
            jax.ShapeDtypeStruct((C, R), BF16),
            jax.ShapeDtypeStruct((F, T), BF16),
        ),
        in_specs=[pl.BlockSpec(memory_space=pl.ANY)] * 4,
        out_specs=[pl.BlockSpec(memory_space=pl.ANY)] * 2,
        scratch_shapes=scratch,
        compiler_params=pltpu.CompilerParams(
            collective_id=level, has_side_effects=True, vmem_limit_bytes=56 * 2**20
        ),
        cost_estimate=pl.CostEstimate(
            flops=20 * T * 8 * F * C, bytes_accessed=6 * R * C, transcendentals=2 * T * C
        ),
    )(tokens, gate_weight, up_weight, hidden_grad)


def shards(tokens, gate_weight, up_weight, hidden_grad, step_index):
    devices = lax.axis_size("dp")
    levels = (devices // 4).bit_length() - 1
    branches = [functools.partial(call_step, level, devices) for level in range(levels)]
    averaged_up, input_grad = lax.switch(
        step_index[0] % levels, branches, tokens.T, gate_weight.T, up_weight.T, hidden_grad.T
    )
    return averaged_up.T, input_grad.T


def solution(mesh):
    placed = (P("dp", "tensor"), P("dp", "tensor"), P("dp", "tensor"), P("dp", "tensor"), P())
    return jax.shard_map(
        shards,
        mesh=mesh,
        in_specs=placed,
        out_specs=(P("dp", "tensor"), P("dp", "tensor")),
        check_vma=False,
    )
```

time: 285 us -> 135 us (0.47)
  the two profiles are of different devices: /device:TPU:1 before, /device:TPU:8 now
where the time goes in v2:
time: 135 us; the launch traced here: 134 us
  Pallas kernels  131 us (97%)
  local copies, waits for them, and re-layouts  1.66 us (1%)
    pallas_call x1, Pallas kernels, call_step(): pl.pallas_call(functools.partial(step_kernel, level, groups_dp), out_shap...  131 us

profile of v2, /device:TPU:8, one launch (start us, length us, event | category | flops | bytes accessed | tf_op | source)
XLA Modules:
  0.0 134.4 jit_solution(4557020311224547092)
XLA Ops:
  1.3 131.4 %conditional.1 = ((bf16[864,640]{1,0:T(8,128)(2,1)S(1)}, bf16[320,256]{1,0:T(8,128)(2,1)S(1)})) conditional(s32[]{:T(128)} %clamp.3, (bf16[320,256]{1,0:T(8,128)(2,1)}, bf16[864,640]{1,0:T(8,128)(2,1)}, bf16[864,640]{1,0:T(8,128)(2,1)}, bf16[864,256]{1,0:T(8,128)(2,1)}) %tuple.44, (bf16[320,256]{1,0:T(8,128)(2,1)}, ...), branch_computations={%region_0.1_spmd, %region_1.2_spmd, %region_2.3_spmd, %region_3.4_... | conditional | flops 11324620800 | bytes 3317768 | solution.py:397
  1.3 131.2 %branch_0_fun.1 = (bf16[864,640]{1,0:T(8,128)(2,1)S(1)}, bf16[320,256]{1,0:T(8,128)(2,1)S(1)}) custom-call(bf16[320,256]{1,0:T(8,128)(2,1)} %get-tuple-element.32.tok, bf16[864,640]{1,0:T(8,128)(2,1)} %get-tuple-element.33.gw, bf16[864,640]{1,0:T(8,128)(2,1)} %get-tuple-element.34.uw, bf16[864,256]{1,0:T(8,128)(2,1)} %get-tuple-element.35.cot), custom_call_target="tpu_custom_call" | custom-call | flops 11324620800 | bytes 3317760 | tf_op jit(solution)/shard_map/cond/branch_0_fun/pallas_call | solution.py:375
  132.7 1.0 copy.18
  133.7 0.7 copy.19
